TPU v7x, 512 devices: a whole 4x4x16 slice. The times are simulated.
512 devices in a mesh: req: 32 (over y, z_lo), head: 16 (over x, z_hi, core).
Axes of the slice: x: 4, y: 4, z: 16 (z_hi: 2, z_lo: 8; z = z_hi * 8 + z_lo), core: 2. Of those that a mesh axis runs over, the one named last changes fastest.
Arguments:
- hidden: bfloat16 [256, 2048], P('req', 'head'), may hold values from -6 to 6
- attn_gain: float32 [2048], replicated, may hold values from 0.1 to 1.9
- q_weight: bfloat16 [2048, 2048], P(None, 'head'), may hold values from -0.125 to 0.125
- gate_weight: bfloat16 [2048, 2048], P(None, 'head'), may hold values from -0.125 to 0.125
- key_value_weight: bfloat16 [2048, 2048], P(None, 'head'), may hold values from -0.125 to 0.125
- q_gain: float32 [128], replicated, may hold values from 0.5 to 1.5
- k_gain: float32 [128], replicated, may hold values from 0.5 to 2
- out_weight: bfloat16 [2048, 2048], P('head'), may hold values from -0.5 to 0.5
- prompt_key_cache: bfloat16 [32, 4096, 8, 128], P('req', 'head'), may hold values from -3.5 to 3.5
- prompt_value_cache: bfloat16 [32, 4096, 8, 128], P('req', 'head'), may hold values from -6 to 6
- tail_key_cache: bfloat16 [32, 4, 256, 8, 128], P('req', None, 'head'), may hold values from -3.5 to 3.5
- tail_value_cache: bfloat16 [32, 4, 256, 8, 128], P('req', None, 'head'), may hold values from -6 to 6
- mlp_gain: float32 [2048], replicated, may hold values from 0.1 to 1.9
- mlp_gate: bfloat16 [2048, 6144], P('req', 'head'), may hold values from -0.125 to 0.125
- mlp_up: bfloat16 [2048, 6144], P('req', 'head'), may hold values from -0.125 to 0.125
- mlp_down: bfloat16 [6144, 2048], P('head'), may hold values from -0.109375 to 0.109375
- final_gain: float32 [2048], P('head'), may hold values from 0.1 to 1.9
- score_weight: float32 [2048], P('head'), may hold values from -0.125 to 0.125
- prompt_lengths: int32 [32], replicated, may hold values from 1 to 4096, 65536 in all
- tail_lengths: int32 [32, 4], replicated, may hold values from 1 to 256, 512 in all within a row
- group_prompt: int32 [32], replicated, may hold values from 0 to 31, each once
Outputs:
- new_hidden: bfloat16 [256, 2048], P('req', 'head')
- score: float32 [256], P('req')
Inputs may be any that keep to these rules, and one draw needn't show every extreme that they name: `group_prompt`: every prompt is held by exactly one group. `prompt_lengths`: one prompt has exactly 4096 prefix tokens. `tail_lengths`: in every prompt one continuation has exactly 256 tail tokens.
All inputs are finite; a program needn't handle non-finite values.
Results may differ from a plain program's by a relative error of at most 0.023.
Values may be sent and summed in bfloat16 or wider, within the bound.
A program may use at most 64 MiB of HBM per device.

v0:
```python
import math
import jax
import jax.numpy as jnp
from jax import lax
from jax.sharding import PartitionSpec as P

EPS = 1e-06
THETA = 1000000.0


def rms_scale(value, gain):
    return value * lax.rsqrt(jnp.mean(value * value, axis=-1, keepdims=True) + EPS) * gain


def rotate(value, position):
    head_width = value.shape[-1]
    half_width = head_width // 2
    frequency = jnp.exp(
        -math.log(THETA) * 2.0 * jnp.arange(half_width, dtype=jnp.float32) / head_width
    )
    angles = position.astype(jnp.float32)[:, None] * frequency[None, :]
    cosine = jnp.cos(angles)[:, None, :]
    sine_part = jnp.sin(angles)[:, None, :]
    first_half = value[..., :half_width]
    second_half = value[..., half_width:]
    return jnp.concatenate(
        [
            first_half * cosine - second_half * sine_part,
            second_half * cosine + first_half * sine_part,
        ],
        axis=-1,
    )


def shards(
    hidden,
    attn_gain,
    q_weight,
    gate_weight,
    key_value_weight,
    q_gain,
    k_gain,
    out_weight,
    prompt_key_cache,
    prompt_value_cache,
    tail_key_cache,
    tail_value_cache,
    mlp_gain,
    mlp_gate,
    mlp_up,
    mlp_down,
    final_gain,
    score_weight,
    prompt_lengths,
    tail_lengths,
    group_prompt,
):
    head_count = lax.axis_size("head")
    group_count = lax.axis_size("req")
    group_id = lax.axis_index("req")
    head_place = lax.axis_index("head")
    count_of_rows = hidden.shape[0]
    model_width = attn_gain.shape[0]
    head_width = q_gain.shape[0]
    own_heads = q_weight.shape[1] // head_width
    all_heads = own_heads * head_count
    block_count = key_value_weight.shape[1] // head_width
    kv_heads = block_count * head_count // 2
    sharing_count = all_heads // kv_heads
    cont_count = tail_lengths.shape[1]
    new_count = count_of_rows // cont_count
    score_scale = 1.0 / math.sqrt(head_width)
    slot_ids = jnp.arange(group_count, dtype=jnp.int32)
    prompt_id = jnp.sum(jnp.where(slot_ids == group_id, group_prompt, 0))
    prompt_len = jnp.sum(jnp.where(slot_ids == prompt_id, prompt_lengths, 0))
    tail_row = jnp.sum(jnp.where((slot_ids == prompt_id)[:, None], tail_lengths, 0), axis=0)
    owner_group = jnp.sum(
        jnp.where(group_prompt[None, :] == slot_ids[:, None], slot_ids[None, :], 0), axis=1
    )
    position = (
        prompt_len + tail_row[:, None] + jnp.arange(new_count, dtype=jnp.int32)[None, :]
    ).reshape(count_of_rows)
    whole_rows = lax.all_gather(hidden, "head", axis=1, tiled=True)
    block_rows = whole_rows.astype(jnp.float32)
    normalized_hidden = rms_scale(block_rows, attn_gain).astype(jnp.bfloat16)
    gate_pre = jnp.dot(normalized_hidden, gate_weight, preferred_element_type=jnp.float32)
    query_rows = jnp.dot(normalized_hidden, q_weight, preferred_element_type=jnp.float32).reshape(
        count_of_rows, own_heads, head_width
    )
    query_rows = rotate(rms_scale(query_rows, q_gain), position).astype(jnp.bfloat16)
    projected_rows = jnp.dot(
        normalized_hidden, key_value_weight, preferred_element_type=jnp.float32
    ).reshape(count_of_rows, block_count, head_width)
    is_key = (head_place * block_count + jnp.arange(block_count, dtype=jnp.int32)) % 2 == 0
    keyed = rotate(rms_scale(projected_rows, k_gain), position)
    fresh = jnp.where(is_key[None, :, None], keyed, projected_rows).astype(jnp.bfloat16)
    all_queries, all_fresh = (
        lax.all_gather(
            query_rows.reshape(count_of_rows, own_heads * head_width), "head", axis=1, tiled=True
        ),
        lax.all_gather(
            fresh.reshape(count_of_rows, block_count * head_width), "head", axis=1, tiled=True
        ),
    )
    query_groups = all_queries.reshape(count_of_rows, kv_heads, sharing_count, head_width)
    local_keys = prompt_key_cache[0]
    local_values = prompt_value_cache[0]
    span_length = local_keys.shape[0]
    block_size = min(128, span_length)
    block_total = span_length // block_size
    span_start = head_place * span_length

    def prefix_block(block_id, sums):
        numer_acc, total_acc = sums
        key_block = lax.dynamic_slice_in_dim(local_keys, block_id * block_size, block_size, 0)
        value_block = lax.dynamic_slice_in_dim(local_values, block_id * block_size, block_size, 0)
        scores = (
            jnp.einsum(
                "rkgd,tkd->rkgt", query_groups, key_block, preferred_element_type=jnp.float32
            )
            * score_scale
        )
        slot_pos = span_start + block_id * block_size + jnp.arange(block_size, dtype=jnp.int32)
        attention_weights = jnp.where(
            slot_pos[None, None, None, :] < prompt_len, jnp.exp(scores), 0.0
        )
        numer_acc = numer_acc + jnp.einsum(
            "rkgt,tkd->rkgd",
            attention_weights.astype(jnp.bfloat16),
            value_block,
            preferred_element_type=jnp.float32,
        )
        return (numer_acc, total_acc + jnp.sum(attention_weights, axis=-1))

    start_sums = (
        jnp.zeros((count_of_rows, kv_heads, sharing_count, head_width), jnp.float32),
        jnp.zeros((count_of_rows, kv_heads, sharing_count), jnp.float32),
    )
    numerator, denominator = lax.fori_loop(0, block_total, prefix_block, start_sums)
    continuation_rows = query_groups.reshape(
        cont_count, new_count, kv_heads, sharing_count, head_width
    )
    tkeys = tail_key_cache[0]
    tail_value_rows = tail_value_cache[0]
    tail_span = tkeys.shape[1]
    scores = (
        jnp.einsum(
            "cjkgd,ctkd->cjkgt", continuation_rows, tkeys, preferred_element_type=jnp.float32
        )
        * score_scale
    )
    tail_pos = head_place * tail_span + jnp.arange(tail_span, dtype=jnp.int32)
    tail_live = tail_pos[None, :] < tail_row[:, None]
    attention_weights = jnp.where(tail_live[:, None, None, None, :], jnp.exp(scores), 0.0)
    numerator = numerator + jnp.einsum(
        "ihbyw,iwbs->ihbys",
        attention_weights.astype(jnp.bfloat16),
        tail_value_rows,
        preferred_element_type=jnp.float32,
    ).reshape(count_of_rows, kv_heads, sharing_count, head_width)
    denominator = denominator + jnp.sum(attention_weights, axis=-1).reshape(
        count_of_rows, kv_heads, sharing_count
    )
    numerator = numerator.reshape(count_of_rows, all_heads, head_width)
    denominator = denominator.reshape(count_of_rows, all_heads)
    numer_sum, total_sum = lax.psum((numerator, denominator), "head")
    numer_own = lax.dynamic_slice_in_dim(numer_sum, head_place * own_heads, own_heads, 1)
    total_own = lax.dynamic_slice_in_dim(total_sum, head_place * own_heads, own_heads, 1)
    fresh_all = all_fresh.reshape(count_of_rows, kv_heads, 2, head_width)
    own_kv = max(own_heads // sharing_count, 1)
    per_kv = own_heads // own_kv
    nearby = lax.dynamic_slice_in_dim(fresh_all, head_place * own_heads // sharing_count, own_kv, 1)
    own_queries = query_rows.reshape(cont_count, new_count, own_kv, per_kv, head_width)
    recent_key_rows = nearby[:, :, 0].reshape(cont_count, new_count, own_kv, head_width)
    recent_value_rows = nearby[:, :, 1].reshape(cont_count, new_count, own_kv, head_width)
    scores = (
        jnp.einsum(
            "cjkgd,cukd->cjkgu", own_queries, recent_key_rows, preferred_element_type=jnp.float32
        )
        * score_scale
    )
    causal = (
        jnp.arange(new_count, dtype=jnp.int32)[None, :]
        <= jnp.arange(new_count, dtype=jnp.int32)[:, None]
    )
    attention_weights = jnp.where(causal[None, :, None, None, :], jnp.exp(scores), 0.0)
    numer_own = numer_own + jnp.einsum(
        "bfmne,beml->bfmnl",
        attention_weights.astype(jnp.bfloat16),
        recent_value_rows,
        preferred_element_type=jnp.float32,
    ).reshape(count_of_rows, own_heads, head_width)
    total_own = total_own + jnp.sum(attention_weights, axis=-1).reshape(count_of_rows, own_heads)
    attention = (numer_own / total_own[..., None]).reshape(count_of_rows, own_heads * head_width)
    gated = (attention * jax.nn.sigmoid(gate_pre)).astype(jnp.bfloat16)
    mixed = lax.psum(jnp.dot(gated, out_weight, preferred_element_type=jnp.float32), "head")
    attended = (block_rows + mixed).astype(jnp.bfloat16)
    col_width = model_width // head_count
    wide_rows = attended.astype(jnp.float32)
    mlp_in = rms_scale(wide_rows, mlp_gain).astype(jnp.bfloat16)
    column_in = lax.all_to_all(mlp_in, "req", split_axis=1, concat_axis=0, tiled=True)
    gate_part = jnp.dot(column_in, mlp_gate, preferred_element_type=jnp.float32)
    up_part = jnp.dot(column_in, mlp_up, preferred_element_type=jnp.float32)
    gate_own, up_own = (
        lax.psum_scatter(gate_part, "req", scatter_dimension=0, tiled=True),
        lax.psum_scatter(up_part, "req", scatter_dimension=0, tiled=True),
    )
    act_rows = (jax.nn.silu(gate_own) * up_own).astype(jnp.bfloat16)
    down_part = jnp.dot(act_rows, mlp_down, preferred_element_type=jnp.float32)
    down_total = lax.psum(down_part, "head")
    added = lax.dynamic_slice_in_dim(down_total, head_place * col_width, col_width, 1)
    residual = lax.dynamic_slice_in_dim(wide_rows, head_place * col_width, col_width, 1)
    finished = (residual + added).astype(jnp.bfloat16)
    everyone = lax.all_gather(finished, "req", axis=0, tiled=True)
    my_owner = jnp.sum(jnp.where(slot_ids == group_id, owner_group, 0))
    new_hidden = lax.dynamic_slice_in_dim(everyone, my_owner * count_of_rows, count_of_rows, 0)
    final_rows = new_hidden.astype(jnp.float32)
    squares, product = lax.psum(
        (
            jnp.sum(final_rows * final_rows, axis=-1),
            jnp.sum(final_rows * final_gain * score_weight, axis=-1),
        ),
        "head",
    )
    score = product * lax.rsqrt(squares / model_width + EPS)
    return (new_hidden, score)


def solution(mesh):
    return jax.shard_map(
        shards,
        mesh=mesh,
        in_specs=(
            P("req", "head"),
            P(),
            P(None, "head"),
            P(None, "head"),
            P(None, "head"),
            P(),
            P(),
            P("head", None),
            P("req", "head", None, None),
            P("req", "head", None, None),
            P("req", None, "head", None, None),
            P("req", None, "head", None, None),
            P(),
            P("req", "head"),
            P("req", "head"),
            P("head", None),
            P("head"),
            P("head"),
            P(),
            P(),
            P(),
        ),
        out_specs=(P("req", "head"), P("req")),
        check_vma=False,
    )
```

profile of v0, /device:TPU:1, one launch (start us, length us, event | category | flops | bytes accessed | tf_op | source)
XLA Modules:
  0.0 1502.3 jit_solution(17086110039047880849)
XLA Ops:
  7.3 51.2 %all_gather.12 = bf16[8,2048]{1,0:T(8,128)(2,1)S(1)} all-gather(bf16[8,128]{1,0:T(8,128)(2,1)} %param.23), channel_id=1, replica_groups=mesh['req'=32,'head'=16] {'head'}, dimensions={1}, use_global_device_ids=true | all-gather | bytes 34816 | tf_op jit(solution)/shard_map/all_gather | solution.py:83
  58.4 0.1 fusion.23
  58.6 0.8 select_reduce_fusion
  59.3 1.3 fusion.70
  60.6 0.6 iota_compare_fusion.2
  61.3 2.0 select_reduce_fusion.2
  63.3 0.8 select_reduce_fusion.1
  64.1 0.7 broadcast_add_fusion
  64.8 0.1 add_convert_fusion.1
  64.9 0.1 convert_element_type.64
  65.0 1.4 multiply_reduce_fusion.2
  66.4 0.7 multiply_bitcast_fusion.1
  67.1 0.1 fusion.50
  67.2 0.1 pad_maximum_fusion
  67.3 33.8 %all_gather.13 = bf16[8,2048]{1,0:T(8,128)(2,1)S(1)} all-gather(bf16[8,128]{1,0:T(8,128)(2,1)S(1)} %pad_maximum_fusion), channel_id=1, replica_groups=mesh['req'=32,'head'=16] {'head'}, dimensions={1}, use_global_device_ids=true | all-gather | bytes 34816 | tf_op jit(solution)/shard_map/all_gather | solution.py:98
  101.1 1.4 copy_bitcast_fusion
  102.6 2.6 while.16
  102.6 0.8 add_compare_fusion.2
  103.3 0.3 fusion.110
  103.7 0.2 fusion.111
  103.9 0.7 add_compare_fusion.2
  104.6 0.3 fusion.110
  105.0 0.2 fusion.111
  105.2 0.1 broadcast_compare_fusion
  105.3 0.3 fusion.85
  105.6 1.1 convolution_bitcast_fusion.1
  106.8 0.6 copy.83
  107.6 0.3 multiply_reduce_fusion.1
  107.9 0.1 multiply_bitcast_fusion
  108.0 0.1 fusion.54
  108.1 0.1 fusion.57
  108.2 43.8 %all_gather.14 = bf16[8,2048]{1,0:T(8,128)(2,1)S(1)} all-gather(bf16[8,128]{1,0:T(8,128)(2,1)S(1)} %fusion.57), channel_id=1, replica_groups=mesh['req'=32,'head'=16] {'head'}, dimensions={1}, use_global_device_ids=true | all-gather | bytes 34816 | tf_op jit(solution)/shard_map/all_gather | solution.py:101
  152.1 0.2 fusion.14
  152.3 0.1 copy.84
  152.4 0.1 fusion.66
  152.4 0.1 fusion.68
  152.5 0.1 copy.90
  152.6 0.1 reshape.317
  152.7 0.1 copy.88
  152.8 0.1 copy.87
  152.9 0.1 copy.89
  153.0 62.0 %psum.43 = f32[8,16]{0,1:T(8,128)S(1)} all-reduce(f32[8,16]{0,1:T(8,128)S(1)} %bitcast.127), channel_id=1, replica_groups=mesh['req'=32,'head'=16] {'head'}, use_global_device_ids=true, to_apply=%region_11.12 | all-reduce | flops 128 | bytes 1024 | tf_op jit(solution)/shard_map/psum | solution.py:166
  215.0 0.1 copy.86
  215.1 0.1 fusion.88
  215.2 132.7 %all-reduce.9.cloned.1.call-done = f32[8,16,128]{2,0,1:T(8,128)} async-done(((f32[8,16,128]{2,0,1:T(8,128)}), f32[8,16,128]{2,0,1:T(8,128)}) %all-reduce.9.cloned.1.call-update) | async-done | bytes 65552 | tf_op jit(solution)/shard_map/psum | solution.py:166
  347.9 1.7 fusion.20
  349.7 242.6 %all-reduce.11.cloned.1.call-done = f32[8,2048]{1,0:T(8,128)} async-done(((f32[8,2048]{1,0:T(8,128)}), f32[8,2048]{1,0:T(8,128)}) %all-reduce.11.cloned.1.call-update) | async-done | bytes 65552 | tf_op jit(solution)/shard_map/psum | solution.py:196
  592.3 1.0 multiply_reduce_fusion
  593.3 0.1 multiply_convert_fusion
  593.4 0.1 all_to_all.14
  593.6 0.1 reshape.325
  593.7 16.2 %all_to_all.19 = bf16[32,2,256]{2,1,0:T(2,128)(2,1)S(1)} all-to-all(bf16[32,2,256]{2,1,0:T(2,128)(2,1)S(1)} %reshape.325), channel_id=1, replica_groups=mesh['req'=32,'head'=16] {'req'}, dimensions={0} | all-to-all | bytes 65536 | tf_op jit(solution)/shard_map/all_to_all | solution.py:201
  609.9 0.1 reshape.326
  610.1 0.9 fusion.27
  611.0 1.0 fusion.29
  612.0 1.3 dynamic-slice
  613.9 428.9 %all-reduce.15.cloned.1.call-done = (f32[256,384]{1,0:T(8,128)}, f32[256,384]{1,0:T(8,128)}) async-done(((f32[256,384]{1,0:T(8,128)}, f32[256,384]{1,0:T(8,128)}), (f32[256,384]{1,0:T(8,128)}, f32[256,384]{1,0:T(8,128)})) %all-reduce.15.cloned.1.call-update) | async-done | bytes 786448
  1042.8 1.7 fusion.35
  1045.2 263.3 %all-reduce.13.cloned.1.call-done = f32[8,2048]{1,0:T(8,128)} async-done(((f32[8,2048]{1,0:T(8,128)}), f32[8,2048]{1,0:T(8,128)}) %all-reduce.13.cloned.1.call-update) | async-done | bytes 65552 | tf_op jit(solution)/shard_map/psum | solution.py:210
  1308.5 0.7 add_convert_fusion
  1309.2 101.1 %all_gather.15 = bf16[256,128]{1,0:T(8,128)(2,1)S(1)} all-gather(bf16[8,128]{1,0:T(8,128)(2,1)S(1)} %add_convert_fusion), channel_id=1, replica_groups=mesh['req'=32,'head'=16] {'req'}, dimensions={0}, use_global_device_ids=true | all-gather | bytes 67584 | tf_op jit(solution)/shard_map/all_gather | solution.py:214
  1410.2 0.7 fusion.48
  1411.0 84.3 %all-reduce.3 = (f32[8]{0:T(128)S(1)}, f32[8]{0:T(128)S(1)}) all-reduce(f32[8]{0:T(128)S(1)} %get-tuple-element.172, f32[8]{0:T(128)S(1)} %get-tuple-element.171), channel_id=1, replica_groups=mesh['req'=32,'head'=16] {'head'}, use_global_device_ids=true, to_apply=%region_21.22 | all-reduce | flops 16 | bytes 128 | tf_op jit(solution)/shard_map/psum | solution.py:218
  1495.3 0.5 rsqrt_multiply_fusion
  (50 shorter events, 0.5 us)
Async XLA Ops:
  7.2 1035.7 %copy-start = (bf16[384,2048]{1,0:T(8,128)(2,1)S(1)}, bf16[384,2048]{1,0:T(8,128)(2,1)}, u32[]{:S(2)}) copy-start(bf16[384,2048]{1,0:T(8,128)(2,1)} %param.38) | copy-start | bytes 4718596
  7.2 340.7 %all-reduce.9.cloned.1.call-start = ((), (), s32[]{:S(2)}) async-start(), calls=%async_computation.1 | async-start | bytes 131072 | tf_op jit(solution)/shard_map/psum | solution.py:166
  102.5 2.8 copy-start.11
  102.5 5.0 copy-start.3
  102.5 5.0 copy-start.4
  105.2 2.8 copy-start.8
  105.2 242.7 %copy-start.1 = (bf16[128,2048]{1,0:T(8,128)(2,1)S(1)}, bf16[128,2048]{1,0:T(8,128)(2,1)}, u32[]{:S(2)}) copy-start(bf16[128,2048]{1,0:T(8,128)(2,1)} %param.30) | copy-start | bytes 1572868
  105.2 242.7 %copy-start.2 = (bf16[2048,128]{1,0:T(8,128)(2,1)S(1)}, bf16[2048,128]{1,0:T(8,128)(2,1)}, u32[]{:S(2)}) copy-start(bf16[2048,128]{1,0:T(8,128)(2,1)} %param.26) | copy-start | bytes 1572868
  105.6 487.7 %copy-start.7 = (f32[2048]{0:T(1024)S(1)}, f32[2048]{0:T(1024)}, u32[]{:S(2)}) copy-start(f32[2048]{0:T(1024)} %param.35) | copy-start | bytes 24580
  106.8 503.3 %copy-start.5 = (bf16[64,384]{1,0:T(8,128)(2,1)S(1)}, bf16[64,384]{1,0:T(8,128)(2,1)}, u32[]{:S(2)}) copy-start(bf16[64,384]{1,0:T(8,128)(2,1)} %param.37) | copy-start | bytes 147460
  107.4 484.9 %all-reduce.11.cloned.1.call-start = ((), (), s32[]{:S(2)}) async-start(), calls=%async_computation.2 | async-start | bytes 131072 | tf_op jit(solution)/shard_map/psum | solution.py:196
  107.6 503.4 %copy-start.6 = (bf16[64,384]{1,0:T(8,128)(2,1)S(1)}, bf16[64,384]{1,0:T(8,128)(2,1)}, u32[]{:S(2)}) copy-start(bf16[64,384]{1,0:T(8,128)(2,1)} %param.36) | copy-start | bytes 147460
  349.7 693.2 %all-reduce.15.cloned.1.call-start = ((), (), s32[]{:S(2)}) async-start(), calls=%async_computation.4 | async-start | bytes 1572864
  611.0 799.3 %copy-start.9 = (f32[128]{0:T(128)S(1)}, f32[128]{0:T(128)}, u32[]{:S(2)}) copy-start(f32[128]{0:T(128)} %param.40) | copy-start | bytes 1540
  611.0 799.3 %copy-start.10 = (f32[128]{0:T(128)S(1)}, f32[128]{0:T(128)}, u32[]{:S(2)}) copy-start(f32[128]{0:T(128)} %param.39) | copy-start | bytes 1540
  612.0 696.5 %all-reduce.13.cloned.1.call-start = ((), (), s32[]{:S(2)}) async-start(), calls=%async_computation.3 | async-start | bytes 131072 | tf_op jit(solution)/shard_map/psum | solution.py:210
Sparse Core Ops, SparseCore 0:
  107.6 240.3 all-reduce.8
  351.1 241.2 all-reduce.10
  612.1 430.6 all-reduce.14
  1045.9 262.5 all-reduce.12
where the time goes:
time: 1500 us
  waiting for transfers between devices  1070 us (71%)
  blocking collectives  392 us (26%)
  between operations  15.4 us (1%)
    unnamed x5, waiting for transfers between devices  429 us
    psum x1, waiting for transfers between devices, shards(): down_total = lax.psum(down_part, 'head')  263 us
    psum x1, waiting for transfers between devices, shards(): lax.psum(jnp.dot(gated, out_weight, preferred_element_type=jnp.float32),...  243 us
    psum x1, waiting for transfers between devices, shards(): numer_sum, total_sum = lax.psum((numerator, denominator), 'head')  133 us
    all_gather x1, blocking collectives, shards(): everyone = lax.all_gather(finished, 'req', axis=0, tiled=True)  101 us
    psum x1, blocking collectives, shards(): lax.psum((jnp.sum(final_rows * final_rows, axis=-1), jnp.sum(final_rows *...  84.3 us
    psum x1, blocking collectives, shards(): numer_sum, total_sum = lax.psum((numerator, denominator), 'head')  62 us
    all_gather x1, blocking collectives, shards(): whole_rows = lax.all_gather(hidden, 'head', axis=1, tiled=True)  51.2 us
  transfers between devices with their start and end apart: 4, of which 4 were waited for; matrix products, arithmetic and copies ran while one was open for 0% of the time, Pallas kernels for 0%

commit v1 on v0

--- a/solution.py
+++ b/solution.py
@@ -207,7 +207,8 @@
     )
     act_rows = (jax.nn.silu(gate_own) * up_own).astype(jnp.bfloat16)
     down_part = jnp.dot(act_rows, mlp_down, preferred_element_type=jnp.float32)
-    down_total = lax.psum(down_part, "head")
+    parts = lax.all_gather(down_part, "head")
+    down_total = jnp.sum(parts, axis=0)
     added = lax.dynamic_slice_in_dim(down_total, head_place * col_width, col_width, 1)
     residual = lax.dynamic_slice_in_dim(wide_rows, head_place * col_width, col_width, 1)
     finished = (residual + added).astype(jnp.bfloat16)

time: 1500 us -> 1330 us (0.89)
  waiting for transfers between devices: 1070 us -> 904 us
    psum x1 -> x0, waiting for transfers between devices: 263 us -> none  [shards(): down_total = lax.psum(down_part, 'head')]
    all_gather x0 -> x1, waiting for transfers between devices: none -> 99.8 us  [shards(): parts = lax.all_gather(down_part, 'head')]
where the time goes in v1:
time: 1330 us
  waiting for transfers between devices  904 us (68%)
  blocking collectives  383 us (29%)
  between operations  15.4 us (1%)
    unnamed x5, waiting for transfers between devices  429 us
    psum x1, waiting for transfers between devices, shards(): lax.psum(jnp.dot(gated, out_weight, preferred_element_type=jnp.float32),...  243 us
    psum x1, waiting for transfers between devices, shards(): numer_sum, total_sum = lax.psum((numerator, denominator), 'head')  133 us
    all_gather x1, blocking collectives, shards(): everyone = lax.all_gather(finished, 'req', axis=0, tiled=True)  100 us
    all_gather x1, waiting for transfers between devices, shards(): parts = lax.all_gather(down_part, 'head')  99.8 us
    psum x1, blocking collectives, shards(): lax.psum((jnp.sum(final_rows * final_rows, axis=-1), jnp.sum(final_rows *...  75.5 us
    psum x1, blocking collectives, shards(): numer_sum, total_sum = lax.psum((numerator, denominator), 'head')  62 us
    all_gather x1, blocking collectives, shards(): whole_rows = lax.all_gather(hidden, 'head', axis=1, tiled=True)  51.2 us
  transfers between devices with their start and end apart: 4, of which 4 were waited for; matrix products, arithmetic and copies ran while one was open for 0% of the time, Pallas kernels for 0%

profile of v1, /device:TPU:1, one launch (start us, length us, event | category | flops | bytes accessed | tf_op | source)
XLA Modules:
  0.0 1331.1 jit_solution(16153533904254058176)
XLA Ops:
  7.3 51.2 %all_gather.18 = bf16[8,2048]{1,0:T(8,128)(2,1)S(1)} all-gather(bf16[8,128]{1,0:T(8,128)(2,1)} %param.23), channel_id=1, replica_groups=mesh['req'=32,'head'=16] {'head'}, dimensions={1}, use_global_device_ids=true | all-gather | bytes 34816 | tf_op jit(solution)/shard_map/all_gather | solution.py:83
  58.4 0.1 fusion.23
  58.6 0.8 select_reduce_fusion
  59.3 1.3 fusion.70
  60.6 0.6 iota_compare_fusion.2
  61.3 2.0 select_reduce_fusion.2
  63.3 0.8 select_reduce_fusion.1
  64.1 0.7 broadcast_add_fusion
  64.8 0.1 add_convert_fusion.1
  64.9 0.1 convert_element_type.64
  65.0 1.4 multiply_reduce_fusion.2
  66.4 0.7 multiply_bitcast_fusion.1
  67.1 0.1 fusion.50
  67.2 0.1 pad_maximum_fusion
  67.3 33.8 %all_gather.19 = bf16[8,2048]{1,0:T(8,128)(2,1)S(1)} all-gather(bf16[8,128]{1,0:T(8,128)(2,1)S(1)} %pad_maximum_fusion), channel_id=1, replica_groups=mesh['req'=32,'head'=16] {'head'}, dimensions={1}, use_global_device_ids=true | all-gather | bytes 34816 | tf_op jit(solution)/shard_map/all_gather | solution.py:98
  101.1 1.4 copy_bitcast_fusion
  102.5 2.6 while.16
  102.6 0.7 add_compare_fusion.2
  103.3 0.3 fusion.110
  103.7 0.2 fusion.111
  103.9 0.7 add_compare_fusion.2
  104.6 0.3 fusion.110
  104.9 0.2 fusion.111
  105.2 0.1 broadcast_compare_fusion
  105.3 1.3 fusion.85
  106.6 1.1 convolution_bitcast_fusion.1
  107.7 0.6 copy.83
  108.5 0.3 multiply_reduce_fusion.1
  108.9 0.1 multiply_bitcast_fusion
  109.0 0.1 fusion.54
  109.1 0.1 fusion.57
  109.1 43.8 %all_gather.20 = bf16[8,2048]{1,0:T(8,128)(2,1)S(1)} all-gather(bf16[8,128]{1,0:T(8,128)(2,1)S(1)} %fusion.57), channel_id=1, replica_groups=mesh['req'=32,'head'=16] {'head'}, dimensions={1}, use_global_device_ids=true | all-gather | bytes 34816 | tf_op jit(solution)/shard_map/all_gather | solution.py:101
  153.0 0.2 fusion.14
  153.2 0.1 copy.84
  153.3 0.1 fusion.66
  153.4 0.1 fusion.68
  153.5 0.1 copy.90
  153.5 0.1 reshape.317
  153.6 0.1 copy.88
  153.7 0.1 copy.87
  153.8 0.1 copy.89
  153.9 62.0 %psum.36 = f32[8,16]{0,1:T(8,128)S(1)} all-reduce(f32[8,16]{0,1:T(8,128)S(1)} %bitcast.129), channel_id=1, replica_groups=mesh['req'=32,'head'=16] {'head'}, use_global_device_ids=true, to_apply=%region_11.12 | all-reduce | flops 128 | bytes 1024 | tf_op jit(solution)/shard_map/psum | solution.py:166
  215.9 0.1 copy.86
  216.1 0.1 fusion.88
  216.2 132.7 %all-reduce.8.cloned.1.call-done = f32[8,16,128]{2,0,1:T(8,128)} async-done(((f32[8,16,128]{2,0,1:T(8,128)}), f32[8,16,128]{2,0,1:T(8,128)}) %all-reduce.8.cloned.1.call-update) | async-done | bytes 65552 | tf_op jit(solution)/shard_map/psum | solution.py:166
  348.9 1.7 fusion.20
  350.6 242.6 %all-reduce.10.cloned.1.call-done = f32[8,2048]{1,0:T(8,128)} async-done(((f32[8,2048]{1,0:T(8,128)}), f32[8,2048]{1,0:T(8,128)}) %all-reduce.10.cloned.1.call-update) | async-done | bytes 65552 | tf_op jit(solution)/shard_map/psum | solution.py:196
  593.2 1.0 multiply_reduce_fusion
  594.2 0.1 multiply_convert_fusion
  594.3 0.1 all_to_all.14
  594.5 0.1 reshape.326
  594.6 16.2 %all_to_all.19 = bf16[32,2,256]{2,1,0:T(2,128)(2,1)S(1)} all-to-all(bf16[32,2,256]{2,1,0:T(2,128)(2,1)S(1)} %reshape.326), channel_id=1, replica_groups=mesh['req'=32,'head'=16] {'req'}, dimensions={0} | all-to-all | bytes 65536 | tf_op jit(solution)/shard_map/all_to_all | solution.py:201
  610.8 0.1 reshape.327
  611.0 0.9 fusion.27
  611.9 1.0 fusion.29
  613.0 1.3 dynamic-slice
  614.9 429.1 %all-reduce.12.cloned.1.call-done = (f32[256,384]{1,0:T(8,128)}, f32[256,384]{1,0:T(8,128)}) async-done(((f32[256,384]{1,0:T(8,128)}, f32[256,384]{1,0:T(8,128)}), (f32[256,384]{1,0:T(8,128)}, f32[256,384]{1,0:T(8,128)})) %all-reduce.12.cloned.1.call-update) | async-done | bytes 786448
  1044.0 1.7 fusion.35
  1046.3 99.8 %all-gather.3.cloned.1.call-done = f32[128,2048]{1,0:T(8,128)} async-done(((f32[8,2048]{1,0:T(8,128)}), f32[128,2048]{1,0:T(8,128)}) %all-gather.3.cloned.1.call-update) | async-done | bytes 1048592 | tf_op jit(solution)/shard_map/all_gather | solution.py:210
  1146.1 1.3 bitcast_reduce_fusion
  1147.4 100.4 %all_gather.23 = bf16[256,128]{1,0:T(8,128)(2,1)S(1)} all-gather(bf16[8,128]{1,0:T(8,128)(2,1)S(1)} %add_convert_fusion), channel_id=1, replica_groups=mesh['req'=32,'head'=16] {'req'}, dimensions={0}, use_global_device_ids=true | all-gather | bytes 67584 | tf_op jit(solution)/shard_map/all_gather | solution.py:215
  1247.8 0.7 fusion.48
  1248.6 75.5 %all-reduce.3 = (f32[8]{0:T(128)S(1)}, f32[8]{0:T(128)S(1)}) all-reduce(f32[8]{0:T(128)S(1)} %get-tuple-element.172, f32[8]{0:T(128)S(1)} %get-tuple-element.171), channel_id=1, replica_groups=mesh['req'=32,'head'=16] {'head'}, use_global_device_ids=true, to_apply=%region_21.22 | all-reduce | flops 16 | bytes 128 | tf_op jit(solution)/shard_map/psum | solution.py:219
  1324.0 0.5 rsqrt_multiply_fusion
  (49 shorter events, 0.5 us)
Async XLA Ops:
  7.2 1036.8 %copy-start = (bf16[384,2048]{1,0:T(8,128)(2,1)S(1)}, bf16[384,2048]{1,0:T(8,128)(2,1)}, u32[]{:S(2)}) copy-start(bf16[384,2048]{1,0:T(8,128)(2,1)} %param.38) | copy-start | bytes 4718596
  7.2 341.7 %all-reduce.8.cloned.1.call-start = ((), (), s32[]{:S(2)}) async-start(), calls=%async_computation.1 | async-start | bytes 131072 | tf_op jit(solution)/shard_map/psum | solution.py:166
  102.5 6.0 copy-start.3
  102.5 6.0 copy-start.4
  105.2 3.7 copy-start.8
  105.2 243.7 %copy-start.1 = (bf16[128,2048]{1,0:T(8,128)(2,1)S(1)}, bf16[128,2048]{1,0:T(8,128)(2,1)}, u32[]{:S(2)}) copy-start(bf16[128,2048]{1,0:T(8,128)(2,1)} %param.30) | copy-start | bytes 1572868
  105.2 243.7 %copy-start.2 = (bf16[2048,128]{1,0:T(8,128)(2,1)S(1)}, bf16[2048,128]{1,0:T(8,128)(2,1)}, u32[]{:S(2)}) copy-start(bf16[2048,128]{1,0:T(8,128)(2,1)} %param.26) | copy-start | bytes 1572868
  106.6 487.7 %copy-start.7 = (f32[2048]{0:T(1024)S(1)}, f32[2048]{0:T(1024)}, u32[]{:S(2)}) copy-start(f32[2048]{0:T(1024)} %param.35) | copy-start | bytes 24580
  107.7 503.3 %copy-start.5 = (bf16[64,384]{1,0:T(8,128)(2,1)S(1)}, bf16[64,384]{1,0:T(8,128)(2,1)}, u32[]{:S(2)}) copy-start(bf16[64,384]{1,0:T(8,128)(2,1)} %param.37) | copy-start | bytes 147460
  108.4 484.9 %all-reduce.10.cloned.1.call-start = ((), (), s32[]{:S(2)}) async-start(), calls=%async_computation.2 | async-start | bytes 131072 | tf_op jit(solution)/shard_map/psum | solution.py:196
  108.5 503.4 %copy-start.6 = (bf16[64,384]{1,0:T(8,128)(2,1)S(1)}, bf16[64,384]{1,0:T(8,128)(2,1)}, u32[]{:S(2)}) copy-start(bf16[64,384]{1,0:T(8,128)(2,1)} %param.36) | copy-start | bytes 147460
  350.6 693.4 %all-reduce.12.cloned.1.call-start = ((), (), s32[]{:S(2)}) async-start(), calls=%async_computation.4 | async-start | bytes 1572864
  612.9 635.0 %copy-start.9 = (f32[128]{0:T(128)S(1)}, f32[128]{0:T(128)}, u32[]{:S(2)}) copy-start(f32[128]{0:T(128)} %param.40) | copy-start | bytes 1540
  612.9 635.0 %copy-start.10 = (f32[128]{0:T(128)S(1)}, f32[128]{0:T(128)}, u32[]{:S(2)}) copy-start(f32[128]{0:T(128)} %param.39) | copy-start | bytes 1540
  612.9 533.2 %all-gather.3.cloned.1.call-start = ((), (), s32[]{:S(2)}) async-start(), calls=%async_computation.3 | async-start | bytes 1114112 | tf_op jit(solution)/shard_map/all_gather | solution.py:210
Sparse Core Ops, SparseCore 0:
  108.5 240.3 all-reduce.7
  352.0 241.1 all-reduce.9
  613.0 430.9 all-reduce.11
  1047.6 98.4 all-gather.2
